TPU v7x, 256 devices: a whole 4x4x8 slice. The times are simulated.
256 devices in a mesh: east: 8 (over z_hi, core), north: 32 (over y, z_lo, x).
Axes of the slice: x: 4, y: 4, z: 8 (z_hi: 4, z_lo: 2; z = z_hi * 2 + z_lo), core: 2. Of those that a mesh axis runs over, the one named last changes fastest.
Arguments:
- adjoint_start: float32 [5, 128, 1024, 256], P(None, 'east', 'north'), may hold values from -3 to 3
- adjoint_source: float32 [5, 128, 1024, 256], P(None, 'east', 'north'), may hold values from -6 to 6
- base_flow: float32 [3, 128, 1024, 256], P(None, 'east', 'north'), may hold values from -3 to 3
- eddy_visc: float32 [128, 1024, 256], P('east', 'north'), may hold values from 0.1 to 3
- rotor_count: int32 [8, 32], P('east', 'north'), may hold values from 128 to 1024, as said below
- rotor_cell: int32 [8, 32, 1024], P('east', 'north'), may hold values from 0 to 131071
- rotor_turbine: int32 [8, 32, 1024], P('east', 'north'), may hold values from 0 to 383
- rotor_sector: int32 [8, 32, 1024], P('east', 'north'), may hold values from 0 to 7
- rotor_weight: float32 [8, 32, 1024], P('east', 'north'), may hold values from 0.25 to 1
Outputs:
- adjoint_final: float32 [5, 128, 1024, 256], P(None, 'east', 'north')
- thrust_grad: float32 [4, 8, 384], P(None, None, 'north')
Inputs may be any that keep to these rules, and one draw needn't show every extreme that they name: `rotor_count`: an eighth of the tiles (at least one), drawn from the seed, hold 1024 live entries; the others hold 128 to 256.
All inputs are finite; a program needn't handle non-finite values.
Results may differ from a plain program's by a relative error of at most 0.0001.
Values sent between devices are 32-bit elements; how exact they have to be, the bound alone decides.
A program may use at most 192 MiB of HBM per device.

v0:
```python
import jax
import jax.numpy as jnp
from jax import lax
from jax.sharding import PartitionSpec as P

SECT = 8
TURB_DEV = 12


def extended(shard, sides, width):
    for axis, dim in sides:
        size, length = (lax.axis_size(axis), shard.shape[dim])
        up = [(i, (i + 1) % size) for i in range(size - 1)]
        down = [(j, i) for i, j in up]
        last = lax.slice_in_dim(shard, length - width, length, axis=dim)
        leading = lax.slice_in_dim(shard, 0, width, axis=dim)
        before = lax.ppermute(last, axis, up)
        after = lax.ppermute(leading, axis, down)
        shard = jnp.concatenate([before, shard, after], axis=dim)
    return shard


def spread(field):
    return jnp.pad(field, ((0, 0), (0, 0), (0, 0), (1, 1)))


def beside_all(padded):
    total = padded[:, 2:, 1:-1, 1:-1] + padded[:, :-2, 1:-1, 1:-1]
    total = total + padded[:, 1:-1, 2:, 1:-1] + padded[:, 1:-1, :-2, 1:-1]
    return total + padded[:, 1:-1, 1:-1, 2:] + padded[:, 1:-1, 1:-1, :-2]


def slopes(padded):
    return [
        padded[:, 2:, 1:-1, 1:-1] - padded[:, :-2, 1:-1, 1:-1],
        padded[:, 1:-1, 2:, 1:-1] - padded[:, 1:-1, :-2, 1:-1],
        padded[:, 1:-1, 1:-1, 2:] - padded[:, 1:-1, 1:-1, :-2],
    ]


def relax(state_pad, base_pad, source):
    full = spread(state_pad)
    base_full = spread(base_pad)
    centre = full[:, 1:-1, 1:-1, 1:-1]
    base_centre = base_full[:, 1:-1, 1:-1, 1:-1]
    neighbours = beside_all(full)
    diffs = slopes(full)
    velocity_base = base_centre[:3]
    viscous = 1.0 + base_centre[3]
    convect = (
        velocity_base[0] * diffs[0][:3]
        + velocity_base[1] * diffs[1][:3]
        + velocity_base[2] * diffs[2][:3]
    )
    pressure_grad = jnp.stack([diffs[0][3], diffs[1][3], diffs[2][3]])
    velocity = (source[:3] + viscous * neighbours[:3] + 0.5 * convect - 0.5 * pressure_grad) / (
        6.0 * viscous + 1.0
    )
    diverge = diffs[0][0] + diffs[1][1] + diffs[2][2]
    pressure = (source[3] + neighbours[3] - 0.5 * diverge) / 7.0
    curvature = beside_all(base_full[:3]) - 6.0 * velocity_base
    eddy_new = (
        source[4] + viscous * neighbours[4] + 0.25 * jnp.sum(centre[:3] * curvature, axis=0)
    ) / (6.0 * viscous + 2.0)
    return jnp.concatenate([velocity, pressure[None], eddy_new[None]], axis=0)


def shards(
    adjoint_start,
    adjoint_source,
    base_flow,
    eddy_visc,
    rotor_count,
    rotor_cell,
    rotor_turbine,
    rotor_sector,
    rotor_weight,
):
    base_four = jnp.concatenate([base_flow, eddy_visc[None]], axis=0)
    base_pad = extended(base_four, (("east", 1), ("north", 2)), 1)
    state = adjoint_start
    for sweep in range(2):
        state_pad = extended(state, (("east", 1), ("north", 2)), 1)
        state = relax(state_pad, base_pad, adjoint_source)
    cells = rotor_cell.reshape(-1)
    flat_state = state.reshape(5, -1)
    values = flat_state[:, cells]
    chosen = jnp.stack([values[0], values[1], values[2], values[4]])
    upstream = base_flow[0].reshape(-1)[cells]
    slot_count = cells.shape[0]
    live = jnp.arange(slot_count, dtype=jnp.int32) < rotor_count.reshape(-1)[0]
    factor = jnp.where(live, rotor_weight.reshape(-1) * upstream * jnp.abs(upstream), 0.0)
    terms = chosen * factor[None]
    sector_hot = (
        rotor_sector.reshape(-1)[None, :] == jnp.arange(SECT, dtype=jnp.int32)[:, None]
    ).astype(jnp.float32)
    combined = (terms[:, None, :] * sector_hot[None]).reshape(4 * SECT, slot_count)
    turbine_total_count = TURB_DEV * lax.axis_size("north")
    turbine_hot = (
        rotor_turbine.reshape(-1)[:, None]
        == jnp.arange(turbine_total_count, dtype=jnp.int32)[None, :]
    ).astype(jnp.float32)
    partial_grad = jnp.dot(
        combined, turbine_hot, precision=lax.Precision.HIGHEST, preferred_element_type=jnp.float32
    )
    summed = lax.psum(partial_grad, ("east", "north"))
    owned = lax.dynamic_slice_in_dim(summed, lax.axis_index("north") * TURB_DEV, TURB_DEV, 1)
    return (state, owned.reshape(4, SECT, TURB_DEV))


def solution(mesh):
    placed = (
        P(None, "east", "north", None),
        P(None, "east", "north", None),
        P(None, "east", "north", None),
        P("east", "north", None),
        P("east", "north"),
        P("east", "north", None),
        P("east", "north", None),
        P("east", "north", None),
        P("east", "north", None),
    )
    return jax.shard_map(
        shards,
        mesh=mesh,
        in_specs=placed,
        out_specs=(P(None, "east", "north", None), P(None, None, "north")),
        check_vma=False,
    )
```

profile of v0, /device:TPU:1, one launch (start us, length us, event | category | flops | bytes accessed | tf_op | source)
XLA Modules:
  0.0 241.2 jit_solution(15971372391863261522)
XLA Ops:
  0.6 1.9 pad_maximum_fusion.37
  2.5 6.3 %collective-permute-start.5 = (f32[4,1,32,256]{3,2,1,0:T(8,128)}, f32[4,1,32,256]{3,2,1,0:T(8,128)}, u32[]{:S(2)}, u32[]{:S(2)}) collective-permute-start(f32[4,1,32,256]{3,2,1,0:T(8,128)} %get-tuple-element.27), channel_id=1, source_target_pairs={{0,32},{32,64},{64,96},{96,128},{128,160},{160,192},{192,224},{1,3... | collective-permute-start | bytes 393224 | tf_op jit(solution)/shard_map/ppermute | solution.py:17
  8.8 1.9 collective-permute-start.4
  10.7 1.7 fusion.45
  12.5 1.9 collective-permute-start
  14.4 4.5 %collective-permute-start.1 = (f32[5,1,32,256]{3,2,1,0:T(8,128)}, f32[5,1,32,256]{3,2,1,0:T(8,128)S(1)}, u32[]{:S(2)}, u32[]{:S(2)}) collective-permute-start(f32[5,1,32,256]{3,2,1,0:T(8,128)} %get-tuple-element.24), channel_id=1, source_target_pairs={{0,32},{32,64},{64,96},{96,128},{128,160},{160,192},{192,224},{1,3... | collective-permute-start | bytes 491528 | tf_op jit(solution)/shard_map/ppermute | solution.py:17
  19.0 0.9 broadcast_add_fusion
  19.9 1.5 fusion.46
  21.4 0.6 fusion.42
  22.7 1.3 copy.25
  24.0 6.2 %gather_fusion.1 = f32[1024]{0:T(1024)S(1)} fusion(f32[131072]{0:T(1024)S(1)} %bitcast.42, s32[1024]{0:T(1024)S(1)} %broadcast_clamp_fusion), kind=kCustom, calls=%fused_computation.1 | custom fusion | bytes 12288 | tf_op jit(solution)/shard_map/gather | solution.py:89
  30.2 1.1 pad_maximum_fusion.44
  31.2 3.1 %collective-permute-start.7 = (f32[4,18,1,256]{3,2,1,0:T(1,128)S(1)}, f32[4,18,1,256]{3,2,1,0:T(1,128)S(1)}, u32[]{:S(2)}, u32[]{:S(2)}) collective-permute-start(f32[4,18,1,256]{3,2,1,0:T(1,128)S(1)} %get-tuple-element.25), channel_id=1, source_target_pairs={{0,1},{1,2},{2,3},{3,4},{4,5},{5,6},{6,7},{7,8},{8,9},{9,10},{10,1... | collective-permute-start | bytes 221192 | tf_op jit(solution)/shard_map/ppermute | solution.py:17
  34.4 1.3 collective-permute-start.6
  35.7 0.6 fusion.2
  36.5 4.0 %collective-permute-start.3 = (f32[5,18,1,256]{3,2,1,0:T(1,128)S(1)}, f32[5,18,1,256]{3,2,1,0:T(1,128)S(1)}, u32[]{:S(2)}, u32[]{:S(2)}) collective-permute-start(f32[5,18,1,256]{3,2,1,0:T(1,128)S(1)} %get-tuple-element.14), channel_id=1, source_target_pairs={{0,1},{1,2},{2,3},{3,4},{4,5},{5,6},{6,7},{7,8},{8,9},{9,10},{10,1... | collective-permute-start | bytes 276488 | tf_op jit(solution)/shard_map/ppermute | solution.py:17
  40.5 1.3 collective-permute-start.2
  41.8 0.8 slice.359
  42.6 5.5 %select_maximum_fusion.8 = f32[4,18,34,258]{3,2,1,0:T(8,128)S(1)} fusion(f32[4,18,1,256]{3,2,1,0:T(1,128)S(1)} %collective-permute-done.6, f32[4,18,1,256]{3,2,1,0:T(1,128)S(1)} %collective-permute-done.7, f32[4,1,32,256]{3,2,1,0:T(8,128)} %collective-permute-done.4, f32[4,1,32,256]{3,2,1,0:T(8,128)} %collective-permute-done.5, ...), kind=kLoop, calls=%fused_computation.15 | loop fusion | flops 8842176 | bytes 5033088 | tf_op jit(solution)/shard_map/concatenate | solution.py:19
  48.2 3.0 %select_maximum_fusion.6 = f32[5,18,34,258]{3,2,1,0:T(8,128)S(1)} fusion(f32[5,18,1,256]{3,2,1,0:T(1,128)S(1)} %collective-permute-done.2, f32[5,18,32,256]{3,2,1,0:T(8,128)S(1)} %constant_dynamic-update-slice_fusion, f32[5,18,1,256]{3,2,1,0:T(1,128)S(1)} %collective-permute-done.3), kind=kLoop, calls=%fused_computation.12 | loop fusion | flops 6315840 | bytes 6291360 | tf_op jit(solution)/shard_map/concatenate | solution.py:19
  51.3 3.6 %slice_subtract_fusion.1 = (f32[5,16,32,256]{3,2,1,0:T(8,128)S(1)}, f32[5,16,32,256]{3,2,1,0:T(8,128)S(1)}, f32[5,16,32,256]{3,2,1,0:T(8,128)S(1)}) fusion(f32[5,18,34,258]{3,2,1,0:T(8,128)S(1)} %select_maximum_fusion.6, f32[5,18,32,256]{3,2,1,0:T(8,128)S(1)} %constant_dynamic-update-slice_fusion, f32[5,18,1,256]{3,2,1,0:T(1,128)S(1)} %collective-permute-done.3, ...), kind=kLoop, calls=%fused_computation.46 | loop fusion | flops 7208960 | bytes 19189760 | tf_op jit(solution)/shard_map/sub | solution.py:37
  55.0 5.9 %multiply_reduce_fusion = (f32[16,32,256]{2,1,0:T(8,128)}, f32[16,32,256]{2,1,0:T(8,128)}, f32[3,16,32,256]{3,2,1,0:T(8,128)S(1)}) fusion(f32[5,16,32,256]{3,2,1,0:T(8,128)S(1)} %copy-done.2, f32[16,32,256]{2,1,0:T(8,128)S(1)} %copy-done.5, f32[1,16,32,256]{3,2,1,0:T(8,128)S(1)} %slice.361, f32[1,16,32,256]{3,2,1,0:T(8,128)S(1)} %slice.360, ...), kind=kLoop, calls=%fused_computation.92 | loop fusion | flops 14286848 | bytes 21905408 | tf_op jit(solution)/shard_map/reduce_sum | solution.py:63
  60.9 2.0 fusion.37
  63.0 4.7 %collective-permute-start.9 = (f32[5,1,32,256]{3,2,1,0:T(8,128)S(1)}, f32[5,1,32,256]{3,2,1,0:T(8,128)S(1)}, u32[]{:S(2)}, u32[]{:S(2)}) collective-permute-start(f32[5,1,32,256]{3,2,1,0:T(8,128)S(1)} %get-tuple-element.19), channel_id=1, source_target_pairs={{0,32},{32,64},{64,96},{96,128},{128,160},{160,192},{192,224},{1,3... | collective-permute-start | bytes 491528 | tf_op jit(solution)/shard_map/ppermute | solution.py:17
  67.7 1.9 collective-permute-start.8
  69.7 0.3 collective-permute-done.9
  70.0 5.7 %collective-permute-done.8 = f32[5,1,32,256]{3,2,1,0:T(8,128)S(1)} collective-permute-done((f32[5,1,32,256]{3,2,1,0:T(8,128)S(1)}, f32[5,1,32,256]{3,2,1,0:T(8,128)S(1)}, u32[]{:S(2)}, u32[]{:S(2)}) %collective-permute-start.8) | collective-permute-done | bytes 163872 | tf_op jit(solution)/shard_map/ppermute | solution.py:18
  75.8 5.7 %collective-permute-start.11 = (f32[5,18,1,256]{3,2,1,0:T(1,128)S(1)}, f32[5,18,1,256]{3,2,1,0:T(1,128)S(1)}, u32[]{:S(2)}, u32[]{:S(2)}) collective-permute-start(f32[5,18,1,256]{3,2,1,0:T(1,128)S(1)} %get-tuple-element.12), channel_id=1, source_target_pairs={{0,1},{1,2},{2,3},{3,4},{4,5},{5,6},{6,7},{7,8},{8,9},{9,10},{10,1... | collective-permute-start | bytes 276488 | tf_op jit(solution)/shard_map/ppermute | solution.py:17
  81.5 1.3 collective-permute-start.10
  82.8 0.4 fusion.23
  83.3 3.5 %collective-permute-done.10 = f32[5,18,1,256]{3,2,1,0:T(1,128)S(1)} collective-permute-done((f32[5,18,1,256]{3,2,1,0:T(1,128)S(1)}, f32[5,18,1,256]{3,2,1,0:T(1,128)S(1)}, u32[]{:S(2)}, u32[]{:S(2)}) %collective-permute-start.10) | collective-permute-done | bytes 92192 | tf_op jit(solution)/shard_map/ppermute | solution.py:18
  86.8 6.1 %select_maximum_fusion = f32[5,18,34,258]{3,2,1,0:T(8,128)S(1)} fusion(f32[5,18,1,256]{3,2,1,0:T(1,128)S(1)} %collective-permute-done.10, f32[5,18,1,256]{3,2,1,0:T(1,128)S(1)} %collective-permute-done.11, f32[5,1,32,256]{3,2,1,0:T(8,128)S(1)} %collective-permute-done.8, f32[5,1,32,256]{3,2,1,0:T(8,128)S(1)} %collective-permute-done.9, ...), kind=kLoop, calls=%fused_computation.6 | loop fusion | flops 12631680 | bytes 6291360 | tf_op jit(solution)/shard_map/concatenate | solution.py:19
  92.9 0.8 slice_subtract_fusion
  93.7 1.2 fusion.25
  95.0 4.5 %add_add_fusion = f32[5,16,32,256]{3,2,1,0:T(8,128)S(1)} fusion(f32[5,18,34,258]{3,2,1,0:T(8,128)S(1)} %select_maximum_fusion, f32[5,1,32,256]{3,2,1,0:T(8,128)S(1)} %collective-permute-done.8, f32[1,16,32,256]{3,2,1,0:T(8,128)S(1)} %get-tuple-element.10, f32[1,16,32,256]{3,2,1,0:T(8,128)S(1)} %get-tuple-element.9, ...), kind=kLoop, calls=%fused_computation.43 | loop fusion | flops 13762560 | bytes 10997760 | tf_op jit(solution)/shard_map/add | solution.py:30
  99.5 0.7 fusion.31
  100.3 0.5 copy.24
  100.8 0.5 copy.23
  101.4 1.5 fusion.8
  102.8 1.8 pad_maximum_fusion.21
  104.6 1.1 copy.22
  105.7 3.3 %pad_maximum_fusion = f32[5,131072]{1,0:T(8,128)} fusion(f32[1,131072]{1,0:T(1,128)S(1)} %bitcast.53, f32[1,131072]{1,0:T(1,128)S(1)} %bitcast.54, f32[3,131072]{1,0:T(4,128)S(1)} %bitcast.48), kind=kLoop, calls=%fused_computation.21 | loop fusion | flops 1310720 | bytes 5242880 | tf_op jit(solution)/shard_map/concatenate | solution.py:65
  109.0 30.3 %copy.18 = f32[5,131072]{0,1:T(8,128)} copy(f32[5,131072]{1,0:T(8,128)} %pad_maximum_fusion) | data formatting | bytes 5242880 | tf_op jit(solution)/shard_map/concatenate | solution.py:65
  139.3 10.7 %gather_fusion = f32[1024,5]{1,0:T(8,128)S(1)} fusion(f32[5,131072]{0,1:T(8,128)} %copy.18, s32[1024]{0:T(1024)S(1)} %broadcast_clamp_fusion), kind=kCustom, calls=%fused_computation | custom fusion | bytes 45056 | tf_op jit(solution)/shard_map/gather | solution.py:87
  150.0 0.2 slice.384
  150.7 1.6 fusion.22
  152.2 88.3 %psum.7 = f32[32,384]{0,1:T(8,128)S(1)} all-reduce(f32[32,384]{0,1:T(8,128)S(1)} %fusion.22), channel_id=1, replica_groups=mesh['east'=8,'north'=32] {'east','north'}, use_global_device_ids=true, to_apply=%region_2.3 | all-reduce | flops 12288 | bytes 98304 | tf_op jit(solution)/shard_map/psum | solution.py:106
  240.5 0.7 copy.21
  (55 shorter events, 0.9 us)
Async XLA Ops:
  0.6 19.3 %copy-start = (f32[3,16,32,256]{3,2,1,0:T(8,128)S(1)}, f32[3,16,32,256]{3,2,1,0:T(8,128)}, u32[]{:S(2)}) copy-start(f32[3,16,32,256]{3,2,1,0:T(8,128)} %param.11) | copy-start | bytes 4718596
  0.6 18.3 %copy-start.1 = (f32[16,32,256]{2,1,0:T(8,128)S(1)}, f32[16,32,256]{2,1,0:T(8,128)}, u32[]{:S(2)}) copy-start(f32[16,32,256]{2,1,0:T(8,128)} %param.12) | copy-start | bytes 1572868
  2.5 27.6 %collective-permute-start.5 = (f32[4,1,32,256]{3,2,1,0:T(8,128)}, f32[4,1,32,256]{3,2,1,0:T(8,128)}, u32[]{:S(2)}, u32[]{:S(2)}) collective-permute-start(f32[4,1,32,256]{3,2,1,0:T(8,128)} %get-tuple-element.27), channel_id=1, source_target_pairs={{0,32},{32,64},{64,96},{96,128},{128,160},{160,192},{192,224},{1,3... | collective-permute-start | bytes 393224 | tf_op jit(solution)/shard_map/ppermute | solution.py:17
  8.8 21.4 %collective-permute-start.4 = (f32[4,1,32,256]{3,2,1,0:T(8,128)}, f32[4,1,32,256]{3,2,1,0:T(8,128)}, u32[]{:S(2)}, u32[]{:S(2)}) collective-permute-start(f32[4,1,32,256]{3,2,1,0:T(8,128)} %get-tuple-element.28), channel_id=1, source_target_pairs={{32,0},{64,32},{96,64},{128,96},{160,128},{192,160},{224,192},{33,... | collective-permute-start | bytes 393224 | tf_op jit(solution)/shard_map/ppermute | solution.py:18
  12.5 23.2 %collective-permute-start = (f32[5,1,32,256]{3,2,1,0:T(8,128)}, f32[5,1,32,256]{3,2,1,0:T(8,128)S(1)}, u32[]{:S(2)}, u32[]{:S(2)}) collective-permute-start(f32[5,1,32,256]{3,2,1,0:T(8,128)} %get-tuple-element.23), channel_id=1, source_target_pairs={{32,0},{64,32},{96,64},{128,96},{160,128},{192,160},{224,192},{33,... | collective-permute-start | bytes 491528 | tf_op jit(solution)/shard_map/ppermute | solution.py:18
  14.4 7.0 %copy-start.14 = (s32[1,1,1024]{2,1,0:T(1,128)S(1)}, s32[1,1,1024]{2,1,0:T(1,128)}, u32[]{:S(2)}) copy-start(s32[1,1,1024]{2,1,0:T(1,128)} %param.14) | copy-start | bytes 12292
  14.4 7.0 %copy-start.12 = (s32[1,1,1024]{2,1,0:T(1,128)S(1)}, s32[1,1,1024]{2,1,0:T(1,128)}, u32[]{:S(2)}) copy-start(s32[1,1,1024]{2,1,0:T(1,128)} %param.16) | copy-start | bytes 12292
  14.4 21.3 %collective-permute-start.1 = (f32[5,1,32,256]{3,2,1,0:T(8,128)}, f32[5,1,32,256]{3,2,1,0:T(8,128)S(1)}, u32[]{:S(2)}, u32[]{:S(2)}) collective-permute-start(f32[5,1,32,256]{3,2,1,0:T(8,128)} %get-tuple-element.24), channel_id=1, source_target_pairs={{0,32},{32,64},{64,96},{96,128},{128,160},{160,192},{192,224},{1,3... | collective-permute-start | bytes 491528 | tf_op jit(solution)/shard_map/ppermute | solution.py:17
  30.1 5.6 %copy-start.2 = (f32[5,16,32,256]{3,2,1,0:T(8,128)S(1)}, f32[5,16,32,256]{3,2,1,0:T(8,128)}, u32[]{:S(2)}) copy-start(f32[5,16,32,256]{3,2,1,0:T(8,128)} %param.9) | copy-start | bytes 7864324
  31.2 11.4 %collective-permute-start.7 = (f32[4,18,1,256]{3,2,1,0:T(1,128)S(1)}, f32[4,18,1,256]{3,2,1,0:T(1,128)S(1)}, u32[]{:S(2)}, u32[]{:S(2)}) collective-permute-start(f32[4,18,1,256]{3,2,1,0:T(1,128)S(1)} %get-tuple-element.25), channel_id=1, source_target_pairs={{0,1},{1,2},{2,3},{3,4},{4,5},{5,6},{6,7},{7,8},{8,9},{9,10},{10,1... | collective-permute-start | bytes 221192 | tf_op jit(solution)/shard_map/ppermute | solution.py:17
  34.4 8.3 %collective-permute-start.6 = (f32[4,18,1,256]{3,2,1,0:T(1,128)S(1)}, f32[4,18,1,256]{3,2,1,0:T(1,128)S(1)}, u32[]{:S(2)}, u32[]{:S(2)}) collective-permute-start(f32[4,18,1,256]{3,2,1,0:T(1,128)S(1)} %get-tuple-element.26), channel_id=1, source_target_pairs={{1,0},{2,1},{3,2},{4,3},{5,4},{6,5},{7,6},{8,7},{9,8},{10,9},{11,1... | collective-permute-start | bytes 221192 | tf_op jit(solution)/shard_map/ppermute | solution.py:18
  36.3 11.8 %copy-start.3 = (f32[5,16,32,256]{3,2,1,0:T(8,128)}, f32[5,16,32,256]{3,2,1,0:T(8,128)S(1)}, u32[]{:S(2)}) copy-start(f32[5,16,32,256]{3,2,1,0:T(8,128)S(1)} %get-tuple-element.21) | copy-start | bytes 7864324
  36.5 11.7 %collective-permute-start.3 = (f32[5,18,1,256]{3,2,1,0:T(1,128)S(1)}, f32[5,18,1,256]{3,2,1,0:T(1,128)S(1)}, u32[]{:S(2)}, u32[]{:S(2)}) collective-permute-start(f32[5,18,1,256]{3,2,1,0:T(1,128)S(1)} %get-tuple-element.14), channel_id=1, source_target_pairs={{0,1},{1,2},{2,3},{3,4},{4,5},{5,6},{6,7},{7,8},{8,9},{9,10},{10,1... | collective-permute-start | bytes 276488 | tf_op jit(solution)/shard_map/ppermute | solution.py:17
  40.5 7.7 %collective-permute-start.2 = (f32[5,18,1,256]{3,2,1,0:T(1,128)S(1)}, f32[5,18,1,256]{3,2,1,0:T(1,128)S(1)}, u32[]{:S(2)}, u32[]{:S(2)}) collective-permute-start(f32[5,18,1,256]{3,2,1,0:T(1,128)S(1)} %get-tuple-element.15), channel_id=1, source_target_pairs={{1,0},{2,1},{3,2},{4,3},{5,4},{6,5},{7,6},{8,7},{9,8},{10,9},{11,1... | collective-permute-start | bytes 276488 | tf_op jit(solution)/shard_map/ppermute | solution.py:18
  42.6 5.5 %copy-start.10 = (f32[4,18,1,256]{3,2,1,0:T(1,128)}, f32[4,18,1,256]{3,2,1,0:T(1,128)S(1)}, u32[]{:S(2)}) copy-start(f32[4,18,1,256]{3,2,1,0:T(1,128)S(1)} %collective-permute-done.6) | copy-start | bytes 221188
  51.2 3.7 %copy-start.5 = (f32[16,32,256]{2,1,0:T(8,128)S(1)}, f32[16,32,256]{2,1,0:T(8,128)}, u32[]{:S(2)}) copy-start(f32[16,32,256]{2,1,0:T(8,128)} %get-tuple-element.34) | copy-start | bytes 1572868
  51.2 3.7 %copy-start.6 = (f32[16,32,256]{2,1,0:T(8,128)S(1)}, f32[16,32,256]{2,1,0:T(8,128)}, u32[]{:S(2)}) copy-start(f32[16,32,256]{2,1,0:T(8,128)} %get-tuple-element.30) | copy-start | bytes 1572868
  51.2 3.7 %copy-start.7 = (f32[16,32,256]{2,1,0:T(8,128)S(1)}, f32[16,32,256]{2,1,0:T(8,128)}, u32[]{:S(2)}) copy-start(f32[16,32,256]{2,1,0:T(8,128)} %get-tuple-element.31) | copy-start | bytes 1572868
  63.0 6.7 %copy-start.13 = (f32[1,1,1024]{2,1,0:T(1,128)S(1)}, f32[1,1,1024]{2,1,0:T(1,128)}, u32[]{:S(2)}) copy-start(f32[1,1,1024]{2,1,0:T(1,128)} %param.17) | copy-start | bytes 12292
  63.0 7.0 %collective-permute-start.9 = (f32[5,1,32,256]{3,2,1,0:T(8,128)S(1)}, f32[5,1,32,256]{3,2,1,0:T(8,128)S(1)}, u32[]{:S(2)}, u32[]{:S(2)}) collective-permute-start(f32[5,1,32,256]{3,2,1,0:T(8,128)S(1)} %get-tuple-element.19), channel_id=1, source_target_pairs={{0,32},{32,64},{64,96},{96,128},{128,160},{160,192},{192,224},{1,3... | collective-permute-start | bytes 491528 | tf_op jit(solution)/shard_map/ppermute | solution.py:17
  67.7 7.9 %collective-permute-start.8 = (f32[5,1,32,256]{3,2,1,0:T(8,128)S(1)}, f32[5,1,32,256]{3,2,1,0:T(8,128)S(1)}, u32[]{:S(2)}, u32[]{:S(2)}) collective-permute-start(f32[5,1,32,256]{3,2,1,0:T(8,128)S(1)} %get-tuple-element.20), channel_id=1, source_target_pairs={{32,0},{64,32},{96,64},{128,96},{160,128},{192,160},{224,192},{33,... | collective-permute-start | bytes 491528 | tf_op jit(solution)/shard_map/ppermute | solution.py:18
  75.8 7.5 %collective-permute-start.11 = (f32[5,18,1,256]{3,2,1,0:T(1,128)S(1)}, f32[5,18,1,256]{3,2,1,0:T(1,128)S(1)}, u32[]{:S(2)}, u32[]{:S(2)}) collective-permute-start(f32[5,18,1,256]{3,2,1,0:T(1,128)S(1)} %get-tuple-element.12), channel_id=1, source_target_pairs={{0,1},{1,2},{2,3},{3,4},{4,5},{5,6},{6,7},{7,8},{8,9},{9,10},{10,1... | collective-permute-start | bytes 276488 | tf_op jit(solution)/shard_map/ppermute | solution.py:17
  81.5 5.3 %collective-permute-start.10 = (f32[5,18,1,256]{3,2,1,0:T(1,128)S(1)}, f32[5,18,1,256]{3,2,1,0:T(1,128)S(1)}, u32[]{:S(2)}, u32[]{:S(2)}) collective-permute-start(f32[5,18,1,256]{3,2,1,0:T(1,128)S(1)} %get-tuple-element.13), channel_id=1, source_target_pairs={{1,0},{2,1},{3,2},{4,3},{5,4},{6,5},{7,6},{8,7},{9,8},{10,9},{11,1... | collective-permute-start | bytes 276488 | tf_op jit(solution)/shard_map/ppermute | solution.py:18
  95.0 4.6 %copy-start.4 = (f32[5,16,32,256]{3,2,1,0:T(8,128)S(1)}, f32[5,16,32,256]{3,2,1,0:T(8,128)}, u32[]{:S(2)}) copy-start(f32[5,16,32,256]{3,2,1,0:T(8,128)} %param.10) | copy-start | bytes 7864324
  95.0 4.6 %copy-start.9 = (f32[16,32,256]{2,1,0:T(8,128)S(1)}, f32[16,32,256]{2,1,0:T(8,128)}, u32[]{:S(2)}) copy-start(f32[16,32,256]{2,1,0:T(8,128)} %get-tuple-element.2) | copy-start | bytes 1572868
  99.5 1.8 copy-start.8
  109.0 41.6 %copy-start.11 = (f32[8,1024]{1,0:T(8,128)S(1)}, f32[8,1024]{1,0:T(8,128)}, u32[]{:S(2)}) copy-start(f32[8,1024]{1,0:T(8,128)} %fusion.42) | copy-start | bytes 98308
  109.0 41.6 %copy-start.15 = (s32[1,1,1024]{2,1,0:T(1,128)S(1)}, s32[1,1,1024]{2,1,0:T(1,128)}, u32[]{:S(2)}) copy-start(s32[1,1,1024]{2,1,0:T(1,128)} %param.15) | copy-start | bytes 12292
where the time goes:
time: 242 us; the launch traced here: 241 us
  blocking collectives  88.3 us (36%)
  local copies, waits for them, and re-layouts  56.3 us (23%)
  other arithmetic  45.7 us (19%)
  starting transfers between devices  38 us (16%)
  waiting for transfers between devices  9.52 us (4%)
    psum x1, blocking collectives, shards(): summed = lax.psum(partial_grad, ('east', 'north'))  88.3 us
    concatenate x1, local copies, waits for them, and re-layouts, relax(): return jnp.concatenate([velocity, pressure[None], eddy_new[None]], axis=0)  30.3 us
    ppermute x6, starting transfers between devices, extended(): before = lax.ppermute(last, axis, up)  28.4 us
    concatenate x5, other arithmetic, extended(): shard = jnp.concatenate([before, shard, after], axis=dim)  15.8 us
    gather x1, local copies, waits for them, and re-layouts, shards(): values = flat_state[:, cells]  10.7 us
    ppermute x6, starting transfers between devices, extended(): after = lax.ppermute(leading, axis, down)  9.63 us
    ppermute x6, waiting for transfers between devices, extended(): after = lax.ppermute(leading, axis, down)  9.21 us
    gather x1, local copies, waits for them, and re-layouts, shards(): upstream = base_flow[0].reshape(-1)[cells]  6.15 us
  transfers between devices with their start and end apart: 12, of which 3 were waited for; matrix products, arithmetic and copies ran while one was open for 9% of the time, Pallas kernels for 0%

commit v1 on v0

--- a/solution.py
+++ b/solution.py
@@ -103,7 +103,8 @@
     partial_grad = jnp.dot(
         combined, turbine_hot, precision=lax.Precision.HIGHEST, preferred_element_type=jnp.float32
     )
-    summed = lax.psum(partial_grad, ("east", "north"))
+    one_axis = lax.psum(partial_grad, "north")
+    summed = lax.psum(one_axis, "east")
     owned = lax.dynamic_slice_in_dim(summed, lax.axis_index("north") * TURB_DEV, TURB_DEV, 1)
     return (state, owned.reshape(4, SECT, TURB_DEV))
 

time: 242 us -> 342 us (1.41)
  blocking collectives: 88.3 us -> 185 us
    psum x1 -> x2, blocking collectives: 88.3 us -> 185 us  [the longest x1 129 us: shards(): one_axis = lax.psum(partial_grad, 'north')]
  transfers between devices with their start and end apart: 12 -> 12, of which waited for: 3 -> 3; matrix products, arithmetic and copies ran while one was open for 9% -> 6% of each run, Pallas kernels for 0% -> 0%
where the time goes in v1:
time: 342 us; the launch traced here: 341 us
  blocking collectives  185 us (54%)
  local copies, waits for them, and re-layouts  56.6 us (17%)
  other arithmetic  47.9 us (14%)
  starting transfers between devices  38 us (11%)
  waiting for transfers between devices  9.51 us (3%)
    psum x1, blocking collectives, shards(): one_axis = lax.psum(partial_grad, 'north')  129 us
    psum x1, blocking collectives, shards(): summed = lax.psum(one_axis, 'east')  56.2 us
    concatenate x1, local copies, waits for them, and re-layouts, relax(): return jnp.concatenate([velocity, pressure[None], eddy_new[None]], axis=0)  30.3 us
    ppermute x6, starting transfers between devices, extended(): before = lax.ppermute(last, axis, up)  28.4 us
    concatenate x5, other arithmetic, extended(): shard = jnp.concatenate([before, shard, after], axis=dim)  15.6 us
    gather x1, local copies, waits for them, and re-layouts, shards(): values = flat_state[:, cells]  10.7 us
    ppermute x6, starting transfers between devices, extended(): after = lax.ppermute(leading, axis, down)  9.63 us
    ppermute x6, waiting for transfers between devices, extended(): after = lax.ppermute(leading, axis, down)  9.21 us
  transfers between devices with their start and end apart: 12, of which 3 were waited for; matrix products, arithmetic and copies ran while one was open for 6% of the time, Pallas kernels for 0%

profile of v1, /device:TPU:1, one launch (start us, length us, event | category | flops | bytes accessed | tf_op | source)
XLA Modules:
  0.0 340.8 jit_solution(2072387821994143403)
XLA Ops:
  0.6 1.9 pad_maximum_fusion.37
  2.5 6.3 %collective-permute-start.5 = (f32[4,1,32,256]{3,2,1,0:T(8,128)}, f32[4,1,32,256]{3,2,1,0:T(8,128)S(1)}, u32[]{:S(2)}, u32[]{:S(2)}) collective-permute-start(f32[4,1,32,256]{3,2,1,0:T(8,128)} %get-tuple-element.27), channel_id=1, source_target_pairs={{0,32},{32,64},{64,96},{96,128},{128,160},{160,192},{192,224},{1,3... | collective-permute-start | bytes 393224 | tf_op jit(solution)/shard_map/ppermute | solution.py:17
  8.8 1.9 collective-permute-start.4
  10.7 1.8 fusion.45
  12.5 1.9 collective-permute-start
  14.4 4.5 %collective-permute-start.1 = (f32[5,1,32,256]{3,2,1,0:T(8,128)}, f32[5,1,32,256]{3,2,1,0:T(8,128)S(1)}, u32[]{:S(2)}, u32[]{:S(2)}) collective-permute-start(f32[5,1,32,256]{3,2,1,0:T(8,128)} %get-tuple-element.24), channel_id=1, source_target_pairs={{0,32},{32,64},{64,96},{96,128},{128,160},{160,192},{192,224},{1,3... | collective-permute-start | bytes 491528 | tf_op jit(solution)/shard_map/ppermute | solution.py:17
  19.0 1.1 broadcast_add_fusion
  20.1 1.2 fusion.46
  21.4 0.6 fusion.42
  22.9 6.2 %gather_fusion.1 = f32[1024]{0:T(1024)S(1)} fusion(f32[131072]{0:T(1024)S(1)} %bitcast.42, s32[1024]{0:T(1024)S(1)} %broadcast_clamp_fusion), kind=kCustom, calls=%fused_computation.1 | custom fusion | bytes 12288 | tf_op jit(solution)/shard_map/gather | solution.py:89
  29.1 1.0 pad_maximum_fusion.44
  30.1 3.1 collective-permute-start.7
  33.3 1.3 collective-permute-start.6
  34.6 0.6 copy-done.10
  35.3 1.9 fusion.2
  37.2 0.9 constant_dynamic-update-slice_fusion
  38.2 4.0 %collective-permute-start.3 = (f32[5,18,1,256]{3,2,1,0:T(1,128)S(1)}, f32[5,18,1,256]{3,2,1,0:T(1,128)S(1)}, u32[]{:S(2)}, u32[]{:S(2)}) collective-permute-start(f32[5,18,1,256]{3,2,1,0:T(1,128)S(1)} %get-tuple-element.14), channel_id=1, source_target_pairs={{0,1},{1,2},{2,3},{3,4},{4,5},{5,6},{6,7},{7,8},{8,9},{9,10},{10,1... | collective-permute-start | bytes 276488 | tf_op jit(solution)/shard_map/ppermute | solution.py:17
  42.2 1.3 collective-permute-start.2
  43.5 0.8 slice.359
  44.4 5.4 %select_maximum_fusion.8 = f32[4,18,34,258]{3,2,1,0:T(8,128)S(1)} fusion(f32[4,18,1,256]{3,2,1,0:T(1,128)S(1)} %collective-permute-done.6, f32[4,18,1,256]{3,2,1,0:T(1,128)S(1)} %collective-permute-done.7, f32[4,1,32,256]{3,2,1,0:T(8,128)} %collective-permute-done.4, f32[4,1,32,256]{3,2,1,0:T(8,128)S(1)} %copy-done.13, f32[1,16,32,256]{3,2,1,0:T(8,128)S(1)} %bitcast.45, ...), kind=kLoop, calls=%fused_computation.15 | loop fusion | flops 8842176 | bytes 5033088 | tf_op jit(solution)/shard_map/concatenate | solution.py:19
  49.8 3.0 select_maximum_fusion.6
  52.9 4.5 %slice_subtract_fusion.1 = (f32[5,16,32,256]{3,2,1,0:T(8,128)S(1)}, f32[5,16,32,256]{3,2,1,0:T(8,128)S(1)}, f32[5,16,32,256]{3,2,1,0:T(8,128)S(1)}) fusion(f32[5,18,34,258]{3,2,1,0:T(8,128)S(1)} %select_maximum_fusion.6, f32[5,18,32,256]{3,2,1,0:T(8,128)S(1)} %constant_dynamic-update-slice_fusion, f32[5,18,1,256]{3,2,1,0:T(1,128)S(1)} %collective-permute-done.3, ...), kind=kLoop, calls=%fused_computation.46 | loop fusion | flops 7208960 | bytes 19189760 | tf_op jit(solution)/shard_map/sub | solution.py:37
  57.5 5.9 %multiply_reduce_fusion = (f32[16,32,256]{2,1,0:T(8,128)}, f32[16,32,256]{2,1,0:T(8,128)}, f32[3,16,32,256]{3,2,1,0:T(8,128)S(1)}) fusion(f32[5,16,32,256]{3,2,1,0:T(8,128)S(1)} %copy-done.2, f32[16,32,256]{2,1,0:T(8,128)} %get-tuple-element.34, f32[1,16,32,256]{3,2,1,0:T(8,128)S(1)} %slice.361, f32[1,16,32,256]{3,2,1,0:T(8,128)S(1)} %slice.360, ...), kind=kLoop, calls=%fused_computation.92 | loop fusion | flops 14286848 | bytes 21905408 | tf_op jit(solution)/shard_map/reduce_sum | solution.py:63
  63.4 1.9 fusion.37
  65.4 4.7 %collective-permute-start.9 = (f32[5,1,32,256]{3,2,1,0:T(8,128)S(1)}, f32[5,1,32,256]{3,2,1,0:T(8,128)S(1)}, u32[]{:S(2)}, u32[]{:S(2)}) collective-permute-start(f32[5,1,32,256]{3,2,1,0:T(8,128)S(1)} %get-tuple-element.19), channel_id=1, source_target_pairs={{0,32},{32,64},{64,96},{96,128},{128,160},{160,192},{192,224},{1,3... | collective-permute-start | bytes 491528 | tf_op jit(solution)/shard_map/ppermute | solution.py:17
  70.1 1.9 collective-permute-start.8
  72.3 5.7 %collective-permute-done.8 = f32[5,1,32,256]{3,2,1,0:T(8,128)S(1)} collective-permute-done((f32[5,1,32,256]{3,2,1,0:T(8,128)S(1)}, f32[5,1,32,256]{3,2,1,0:T(8,128)S(1)}, u32[]{:S(2)}, u32[]{:S(2)}) %collective-permute-start.8) | collective-permute-done | bytes 163872 | tf_op jit(solution)/shard_map/ppermute | solution.py:18
  78.1 5.7 %collective-permute-start.11 = (f32[5,18,1,256]{3,2,1,0:T(1,128)S(1)}, f32[5,18,1,256]{3,2,1,0:T(1,128)S(1)}, u32[]{:S(2)}, u32[]{:S(2)}) collective-permute-start(f32[5,18,1,256]{3,2,1,0:T(1,128)S(1)} %get-tuple-element.12), channel_id=1, source_target_pairs={{0,1},{1,2},{2,3},{3,4},{4,5},{5,6},{6,7},{7,8},{8,9},{9,10},{10,1... | collective-permute-start | bytes 276488 | tf_op jit(solution)/shard_map/ppermute | solution.py:17
  83.9 1.3 collective-permute-start.10
  85.2 0.4 fusion.23
  85.6 3.5 %collective-permute-done.10 = f32[5,18,1,256]{3,2,1,0:T(1,128)S(1)} collective-permute-done((f32[5,18,1,256]{3,2,1,0:T(1,128)S(1)}, f32[5,18,1,256]{3,2,1,0:T(1,128)S(1)}, u32[]{:S(2)}, u32[]{:S(2)}) %collective-permute-start.10) | collective-permute-done | bytes 92192 | tf_op jit(solution)/shard_map/ppermute | solution.py:18
  89.2 6.1 %select_maximum_fusion = f32[5,18,34,258]{3,2,1,0:T(8,128)S(1)} fusion(f32[5,18,1,256]{3,2,1,0:T(1,128)S(1)} %collective-permute-done.10, f32[5,18,1,256]{3,2,1,0:T(1,128)S(1)} %collective-permute-done.11, f32[5,1,32,256]{3,2,1,0:T(8,128)S(1)} %collective-permute-done.8, f32[5,1,32,256]{3,2,1,0:T(8,128)S(1)} %collective-permute-done.9, ...), kind=kLoop, calls=%fused_computation.6 | loop fusion | flops 12631680 | bytes 6291360 | tf_op jit(solution)/shard_map/concatenate | solution.py:19
  95.2 0.8 slice_subtract_fusion
  96.1 1.2 fusion.25
  97.3 4.5 %add_add_fusion = f32[5,16,32,256]{3,2,1,0:T(8,128)S(1)} fusion(f32[5,18,34,258]{3,2,1,0:T(8,128)S(1)} %select_maximum_fusion, f32[5,1,32,256]{3,2,1,0:T(8,128)S(1)} %collective-permute-done.8, f32[1,16,32,256]{3,2,1,0:T(8,128)S(1)} %get-tuple-element.10, f32[1,16,32,256]{3,2,1,0:T(8,128)S(1)} %get-tuple-element.9, ...), kind=kLoop, calls=%fused_computation.43 | loop fusion | flops 13762560 | bytes 10997760 | tf_op jit(solution)/shard_map/add | solution.py:30
  102.0 0.7 fusion.31
  102.7 0.5 copy.24
  103.2 0.5 copy.23
  103.8 1.5 fusion.8
  105.3 1.8 pad_maximum_fusion.21
  107.1 1.1 copy.22
  108.2 3.4 pad_maximum_fusion
  111.5 30.3 %copy.18 = f32[5,131072]{0,1:T(8,128)} copy(f32[5,131072]{1,0:T(8,128)} %pad_maximum_fusion) | data formatting | bytes 5242880 | tf_op jit(solution)/shard_map/concatenate | solution.py:65
  141.8 10.7 %gather_fusion = f32[1024,5]{1,0:T(8,128)S(1)} fusion(f32[5,131072]{0,1:T(8,128)} %copy.18, s32[1024]{0:T(1024)S(1)} %broadcast_clamp_fusion), kind=kCustom, calls=%fused_computation | custom fusion | bytes 45056 | tf_op jit(solution)/shard_map/gather | solution.py:87
  153.2 1.6 fusion.22
  154.8 129.1 %psum.14 = f32[32,384]{0,1:T(8,128)S(1)} all-reduce(f32[32,384]{0,1:T(8,128)S(1)} %fusion.22), channel_id=1, replica_groups=mesh['east'=8,'north'=32] {'north'}, use_global_device_ids=true, to_apply=%region_2.3 | all-reduce | flops 12288 | bytes 98304 | tf_op jit(solution)/shard_map/psum | solution.py:106
  283.9 56.2 %psum.15 = f32[32,384]{0,1:T(8,128)S(1)} all-reduce(f32[32,384]{0,1:T(8,128)S(1)} %psum.14), channel_id=1, replica_groups=mesh['east'=8,'north'=32] {'east'}, use_global_device_ids=true, to_apply=%region_3.4 | all-reduce | flops 12288 | bytes 98304 | tf_op jit(solution)/shard_map/psum | solution.py:107
  340.1 0.7 copy.21
  (66 shorter events, 1.7 us)
Async XLA Ops:
  0.6 19.5 %copy-start = (f32[3,16,32,256]{3,2,1,0:T(8,128)S(1)}, f32[3,16,32,256]{3,2,1,0:T(8,128)}, u32[]{:S(2)}) copy-start(f32[3,16,32,256]{3,2,1,0:T(8,128)} %param.11) | copy-start | bytes 4718596
  0.6 18.3 %copy-start.1 = (f32[16,32,256]{2,1,0:T(8,128)S(1)}, f32[16,32,256]{2,1,0:T(8,128)}, u32[]{:S(2)}) copy-start(f32[16,32,256]{2,1,0:T(8,128)} %param.12) | copy-start | bytes 1572868
  2.5 26.6 %collective-permute-start.5 = (f32[4,1,32,256]{3,2,1,0:T(8,128)}, f32[4,1,32,256]{3,2,1,0:T(8,128)S(1)}, u32[]{:S(2)}, u32[]{:S(2)}) collective-permute-start(f32[4,1,32,256]{3,2,1,0:T(8,128)} %get-tuple-element.27), channel_id=1, source_target_pairs={{0,32},{32,64},{64,96},{96,128},{128,160},{160,192},{192,224},{1,3... | collective-permute-start | bytes 393224 | tf_op jit(solution)/shard_map/ppermute | solution.py:17
  8.8 20.3 %collective-permute-start.4 = (f32[4,1,32,256]{3,2,1,0:T(8,128)}, f32[4,1,32,256]{3,2,1,0:T(8,128)}, u32[]{:S(2)}, u32[]{:S(2)}) collective-permute-start(f32[4,1,32,256]{3,2,1,0:T(8,128)} %get-tuple-element.28), channel_id=1, source_target_pairs={{32,0},{64,32},{96,64},{128,96},{160,128},{192,160},{224,192},{33,... | collective-permute-start | bytes 393224 | tf_op jit(solution)/shard_map/ppermute | solution.py:18
  12.5 22.8 %collective-permute-start = (f32[5,1,32,256]{3,2,1,0:T(8,128)}, f32[5,1,32,256]{3,2,1,0:T(8,128)}, u32[]{:S(2)}, u32[]{:S(2)}) collective-permute-start(f32[5,1,32,256]{3,2,1,0:T(8,128)} %get-tuple-element.23), channel_id=1, source_target_pairs={{32,0},{64,32},{96,64},{128,96},{160,128},{192,160},{224,192},{33,... | collective-permute-start | bytes 491528 | tf_op jit(solution)/shard_map/ppermute | solution.py:18
  14.4 6.9 %copy-start.19 = (s32[1,1,1024]{2,1,0:T(1,128)S(1)}, s32[1,1,1024]{2,1,0:T(1,128)}, u32[]{:S(2)}) copy-start(s32[1,1,1024]{2,1,0:T(1,128)} %param.14) | copy-start | bytes 12292
  14.4 6.9 %copy-start.17 = (s32[1,1,1024]{2,1,0:T(1,128)S(1)}, s32[1,1,1024]{2,1,0:T(1,128)}, u32[]{:S(2)}) copy-start(s32[1,1,1024]{2,1,0:T(1,128)} %param.16) | copy-start | bytes 12292
  14.4 20.1 %collective-permute-start.1 = (f32[5,1,32,256]{3,2,1,0:T(8,128)}, f32[5,1,32,256]{3,2,1,0:T(8,128)S(1)}, u32[]{:S(2)}, u32[]{:S(2)}) collective-permute-start(f32[5,1,32,256]{3,2,1,0:T(8,128)} %get-tuple-element.24), channel_id=1, source_target_pairs={{0,32},{32,64},{64,96},{96,128},{128,160},{160,192},{192,224},{1,3... | collective-permute-start | bytes 491528 | tf_op jit(solution)/shard_map/ppermute | solution.py:17
  29.1 6.2 %copy-start.2 = (f32[5,16,32,256]{3,2,1,0:T(8,128)S(1)}, f32[5,16,32,256]{3,2,1,0:T(8,128)}, u32[]{:S(2)}) copy-start(f32[5,16,32,256]{3,2,1,0:T(8,128)} %param.9) | copy-start | bytes 7864324
  29.1 5.5 %copy-start.12 = (f32[4,1,32,256]{3,2,1,0:T(8,128)}, f32[4,1,32,256]{3,2,1,0:T(8,128)S(1)}, u32[]{:S(2)}) copy-start(f32[4,1,32,256]{3,2,1,0:T(8,128)S(1)} %collective-permute-done.5) | copy-start | bytes 393220
  30.1 14.2 %collective-permute-start.7 = (f32[4,18,1,256]{3,2,1,0:T(1,128)S(1)}, f32[4,18,1,256]{3,2,1,0:T(1,128)S(1)}, u32[]{:S(2)}, u32[]{:S(2)}) collective-permute-start(f32[4,18,1,256]{3,2,1,0:T(1,128)S(1)} %get-tuple-element.25), channel_id=1, source_target_pairs={{0,1},{1,2},{2,3},{3,4},{4,5},{5,6},{6,7},{7,8},{8,9},{9,10},{10,1... | collective-permute-start | bytes 221192 | tf_op jit(solution)/shard_map/ppermute | solution.py:17
  33.3 11.1 %collective-permute-start.6 = (f32[4,18,1,256]{3,2,1,0:T(1,128)S(1)}, f32[4,18,1,256]{3,2,1,0:T(1,128)S(1)}, u32[]{:S(2)}, u32[]{:S(2)}) collective-permute-start(f32[4,18,1,256]{3,2,1,0:T(1,128)S(1)} %get-tuple-element.26), channel_id=1, source_target_pairs={{1,0},{2,1},{3,2},{4,3},{5,4},{6,5},{7,6},{8,7},{9,8},{10,9},{11,1... | collective-permute-start | bytes 221192 | tf_op jit(solution)/shard_map/ppermute | solution.py:18
  34.6 0.7 copy-start.10
  35.3 9.1 %copy-start.13 = (f32[4,1,32,256]{3,2,1,0:T(8,128)S(1)}, f32[4,1,32,256]{3,2,1,0:T(8,128)}, u32[]{:S(2)}) copy-start(f32[4,1,32,256]{3,2,1,0:T(8,128)} %copy-done.12) | copy-start | bytes 393220
  38.2 11.6 %collective-permute-start.3 = (f32[5,18,1,256]{3,2,1,0:T(1,128)S(1)}, f32[5,18,1,256]{3,2,1,0:T(1,128)S(1)}, u32[]{:S(2)}, u32[]{:S(2)}) collective-permute-start(f32[5,18,1,256]{3,2,1,0:T(1,128)S(1)} %get-tuple-element.14), channel_id=1, source_target_pairs={{0,1},{1,2},{2,3},{3,4},{4,5},{5,6},{6,7},{7,8},{8,9},{9,10},{10,1... | collective-permute-start | bytes 276488 | tf_op jit(solution)/shard_map/ppermute | solution.py:17
  42.2 7.6 %collective-permute-start.2 = (f32[5,18,1,256]{3,2,1,0:T(1,128)S(1)}, f32[5,18,1,256]{3,2,1,0:T(1,128)S(1)}, u32[]{:S(2)}, u32[]{:S(2)}) collective-permute-start(f32[5,18,1,256]{3,2,1,0:T(1,128)S(1)} %get-tuple-element.15), channel_id=1, source_target_pairs={{1,0},{2,1},{3,2},{4,3},{5,4},{6,5},{7,6},{8,7},{9,8},{10,9},{11,1... | collective-permute-start | bytes 276488 | tf_op jit(solution)/shard_map/ppermute | solution.py:18
  44.4 5.4 %copy-start.14 = (f32[4,18,1,256]{3,2,1,0:T(1,128)}, f32[4,18,1,256]{3,2,1,0:T(1,128)S(1)}, u32[]{:S(2)}) copy-start(f32[4,18,1,256]{3,2,1,0:T(1,128)S(1)} %collective-permute-done.7) | copy-start | bytes 221188
  44.4 5.4 %copy-start.15 = (f32[4,18,1,256]{3,2,1,0:T(1,128)}, f32[4,18,1,256]{3,2,1,0:T(1,128)S(1)}, u32[]{:S(2)}) copy-start(f32[4,18,1,256]{3,2,1,0:T(1,128)S(1)} %collective-permute-done.6) | copy-start | bytes 221188
  49.8 3.1 copy-start.11
  65.3 6.7 %copy-start.18 = (f32[1,1,1024]{2,1,0:T(1,128)S(1)}, f32[1,1,1024]{2,1,0:T(1,128)}, u32[]{:S(2)}) copy-start(f32[1,1,1024]{2,1,0:T(1,128)} %param.17) | copy-start | bytes 12292
  65.4 7.0 %collective-permute-start.9 = (f32[5,1,32,256]{3,2,1,0:T(8,128)S(1)}, f32[5,1,32,256]{3,2,1,0:T(8,128)S(1)}, u32[]{:S(2)}, u32[]{:S(2)}) collective-permute-start(f32[5,1,32,256]{3,2,1,0:T(8,128)S(1)} %get-tuple-element.19), channel_id=1, source_target_pairs={{0,32},{32,64},{64,96},{96,128},{128,160},{160,192},{192,224},{1,3... | collective-permute-start | bytes 491528 | tf_op jit(solution)/shard_map/ppermute | solution.py:17
  70.1 7.9 %collective-permute-start.8 = (f32[5,1,32,256]{3,2,1,0:T(8,128)S(1)}, f32[5,1,32,256]{3,2,1,0:T(8,128)S(1)}, u32[]{:S(2)}, u32[]{:S(2)}) collective-permute-start(f32[5,1,32,256]{3,2,1,0:T(8,128)S(1)} %get-tuple-element.20), channel_id=1, source_target_pairs={{32,0},{64,32},{96,64},{128,96},{160,128},{192,160},{224,192},{33,... | collective-permute-start | bytes 491528 | tf_op jit(solution)/shard_map/ppermute | solution.py:18
  78.1 7.5 %collective-permute-start.11 = (f32[5,18,1,256]{3,2,1,0:T(1,128)S(1)}, f32[5,18,1,256]{3,2,1,0:T(1,128)S(1)}, u32[]{:S(2)}, u32[]{:S(2)}) collective-permute-start(f32[5,18,1,256]{3,2,1,0:T(1,128)S(1)} %get-tuple-element.12), channel_id=1, source_target_pairs={{0,1},{1,2},{2,3},{3,4},{4,5},{5,6},{6,7},{7,8},{8,9},{9,10},{10,1... | collective-permute-start | bytes 276488 | tf_op jit(solution)/shard_map/ppermute | solution.py:17
  83.9 5.3 %collective-permute-start.10 = (f32[5,18,1,256]{3,2,1,0:T(1,128)S(1)}, f32[5,18,1,256]{3,2,1,0:T(1,128)S(1)}, u32[]{:S(2)}, u32[]{:S(2)}) collective-permute-start(f32[5,18,1,256]{3,2,1,0:T(1,128)S(1)} %get-tuple-element.13), channel_id=1, source_target_pairs={{1,0},{2,1},{3,2},{4,3},{5,4},{6,5},{7,6},{8,7},{9,8},{10,9},{11,1... | collective-permute-start | bytes 276488 | tf_op jit(solution)/shard_map/ppermute | solution.py:18
  97.3 4.6 %copy-start.3 = (f32[5,16,32,256]{3,2,1,0:T(8,128)S(1)}, f32[5,16,32,256]{3,2,1,0:T(8,128)}, u32[]{:S(2)}) copy-start(f32[5,16,32,256]{3,2,1,0:T(8,128)} %param.10) | copy-start | bytes 7864324
  97.3 4.6 %copy-start.9 = (f32[16,32,256]{2,1,0:T(8,128)S(1)}, f32[16,32,256]{2,1,0:T(8,128)}, u32[]{:S(2)}) copy-start(f32[16,32,256]{2,1,0:T(8,128)} %get-tuple-element.2) | copy-start | bytes 1572868
  101.9 1.9 copy-start.4
  101.9 1.9 copy-start.5
  101.9 1.9 copy-start.6
  101.9 1.9 copy-start.7
  102.0 1.9 copy-start.8
  111.5 41.6 %copy-start.16 = (f32[8,1024]{1,0:T(8,128)S(1)}, f32[8,1024]{1,0:T(8,128)}, u32[]{:S(2)}) copy-start(f32[8,1024]{1,0:T(8,128)} %fusion.42) | copy-start | bytes 98308
  111.5 41.6 %copy-start.20 = (s32[1,1,1024]{2,1,0:T(1,128)S(1)}, s32[1,1,1024]{2,1,0:T(1,128)}, u32[]{:S(2)}) copy-start(s32[1,1,1024]{2,1,0:T(1,128)} %param.15) | copy-start | bytes 12292
